TPU v7x, 256 devices: a whole 4x4x8 slice. The times are simulated.
256 devices in a mesh: row: 64 (over z, y, core), layer: 4 (over x).
Axes of the slice: x: 4, y: 4, z: 8, core: 2. Of those that a mesh axis runs over, the one named last changes fastest.
Arguments:
- weights: bfloat16 [8, 5120, 16384], P('layer', 'row'), may hold values from -46 to 46
- coeffs: bfloat16 [8, 5120, 512], P('layer', 'row'), may hold values from -3 to 3
- basis: bfloat16 [512, 16384], P(None, 'row'), may hold values from -0.25 to 0.25
- sketch_map: bfloat16 [8, 16384, 256], P('layer', 'row'), may hold values from -0.015625 to 0.015625
- ranks: int32 [8], replicated, may hold values from 32 to 256, as said below
Outputs:
- coefficients: float32 [8, 256, 16384], P('layer', None, 'row')
Inputs may be any that keep to these rules, and one draw needn't show every extreme that they name: `ranks`: every rank lies between 32 and 256, and both ends are taken by some layer.
All inputs are finite; a program needn't handle non-finite values.
Results may differ from a plain program's by a relative error of at most 0.0048.
Values may be sent and summed in bfloat16 or wider, within the bound.
No kernel may reach another device: no remote copies, remote signals or barrier semaphores. Data moves between devices by JAX's collectives and lax.ppermute only.
A program may use at most 128 MiB of HBM per device.

v0:
```python
import jax
import jax.numpy as jnp
from jax import lax
from jax.sharding import PartitionSpec as P


def per_device(weights, coeffs, basis, sketch_map, ranks):
    lay_dev = weights.shape[0]
    width = sketch_map.shape[2]
    lowrank = jnp.einsum(
        "lrk,kc->lrc",
        coeffs,
        lax.all_gather(basis, "row", axis=1, tiled=True),
        preferred_element_type=jnp.float32,
    )
    residual_rows = (weights.astype(jnp.float32) - lowrank).astype(jnp.bfloat16)
    residual = lax.all_to_all(residual_rows, "row", split_axis=2, concat_axis=1, tiled=True)
    row_sketch = lax.psum_scatter(
        jnp.einsum("lrc,lcs->rs", residual, sketch_map, preferred_element_type=jnp.float32),
        "row",
        scatter_dimension=0,
        tiled=True,
    )
    row_sketch = lax.psum(row_sketch, "layer")
    gram = lax.psum(jnp.dot(row_sketch.T, row_sketch, precision=lax.Precision.HIGHEST), "row")
    factor = jnp.linalg.cholesky(gram)
    ortho_rows = jax.scipy.linalg.solve_triangular(factor, row_sketch.T, lower=True).T.astype(
        jnp.bfloat16
    )
    ortho = lax.all_gather(ortho_rows, "row", axis=0, tiled=True)
    ranks_here = lax.dynamic_slice_in_dim(ranks, lax.axis_index("layer") * lay_dev, lay_dev)
    projected = jnp.einsum("ds,ldc->lsc", ortho, residual, preferred_element_type=jnp.float32)
    kept_rows = jnp.arange(width, dtype=jnp.int32)[None, :] < ranks_here[:, None]
    return jnp.where(kept_rows[:, :, None], projected, 0.0)


def solution(mesh):
    in_specs = (
        P("layer", "row", None),
        P("layer", "row", None),
        P(None, "row"),
        P("layer", "row", None),
        P(),
    )
    out_specs = P("layer", None, "row")
    return jax.shard_map(
        per_device, mesh=mesh, in_specs=in_specs, out_specs=out_specs, check_vma=False
    )
```

profile of v0, /device:TPU:1, one launch (start us, length us, event | category | flops | bytes accessed | tf_op | source)
XLA Modules:
  0.0 888.1 jit_solution(6241238721937389962)
XLA Ops:
  6.5 0.0 copy-start
  6.5 0.0 all-gather.3.cloned.1.call-start
  6.5 0.7 all-gather.3.cloned.1.call-update
  7.3 0.0 reduce-scatter.2.cloned.1.call-start
  7.3 114.1 %all-gather.3.cloned.1.call-done = bf16[512,16384]{1,0:T(8,128)(2,1)} async-done(((bf16[512,256]{1,0:T(8,128)(2,1)}), bf16[512,16384]{1,0:T(8,128)(2,1)}) %all-gather.3.cloned.1.call-update) | async-done | bytes 16777232 | tf_op jit(solution)/shard_map/all_gather | solution.py:13
  121.4 12.5 %fusion = bf16[2,80,16384]{2,1,0:T(8,128)(2,1)} fusion(bf16[2,80,512]{2,1,0:T(8,128)(2,1)} %param.6, bf16[512,16384]{1,0:T(8,128)(2,1)} %all-gather.3.cloned.1.call-done, bf16[2,80,16384]{2,1,0:T(8,128)(2,1)} %param.5), kind=kOutput, calls=%fused_computation.3 | convolution fusion | flops 2692218880 | bytes 27426816 | tf_op jit(solution)/shard_map/lrk,kc->lrc/dot_general | solution.py:10
  133.9 18.0 %copy.11 = bf16[2,80,16384]{1,0,2:T(2,128)(2,1)} copy(bf16[2,80,16384]{2,1,0:T(8,128)(2,1)} %fusion) | data formatting | bytes 10485760 | tf_op jit(solution)/shard_map/convert_element_type | solution.py:16
  151.9 190.8 %all_to_all.18 = bf16[2,80,16384]{1,0,2:T(2,128)(2,1)} all-to-all(bf16[2,80,16384]{1,0,2:T(2,128)(2,1)} %copy.11), channel_id=1, replica_groups=mesh['row'=64,'layer'=4] {'row'}, dimensions={2} | all-to-all | bytes 10485760 | tf_op jit(solution)/shard_map/all_to_all | solution.py:17
  342.7 17.7 %copy.12 = bf16[2,80,64,256]{3,1,2,0:T(8,128)(2,1)} copy(bf16[2,80,64,256]{1,0,3,2:T(2,128)(2,1)} %bitcast.62) | data formatting | bytes 10485760 | tf_op jit(solution)/shard_map/all_to_all | solution.py:17
  360.4 0.0 copy-done
  360.4 6.3 convolution_bitcast_fusion
  366.7 0.0 copy-start.1
  366.7 0.0 reduce-scatter.2.cloned.1.call-update
  366.8 0.0 all-reduce.4.cloned.1.call-start
  366.8 138.0 %reduce-scatter.2.cloned.1.call-done = f32[80,256]{1,0:T(8,128)} async-done(((f32[5120,256]{1,0:T(8,128)}), f32[80,256]{1,0:T(8,128)}) %reduce-scatter.2.cloned.1.call-update) | async-done | bytes 81936 | tf_op jit(solution)/shard_map/reduce_scatter | solution.py:18
  504.8 0.0 all-reduce.4.cloned.1.call-update
  504.8 0.0 all-reduce.6.cloned.1.call-start
  504.8 49.4 %all-reduce.4.cloned.1.call-done = f32[80,256]{1,0:T(8,128)} async-done(((f32[80,256]{1,0:T(8,128)}), f32[80,256]{1,0:T(8,128)}) %all-reduce.4.cloned.1.call-update) | async-done | bytes 81936 | tf_op jit(solution)/shard_map/psum | solution.py:24
  554.3 2.1 fusion.19
  556.3 0.0 all-reduce.6.cloned.1.call-update
  556.4 0.2 all-gather.5.cloned.1.call-start
  556.6 179.0 %all-reduce.6.cloned.1.call-done = f32[256,256]{0,1:T(8,128)} async-done(((f32[256,256]{0,1:T(8,128)}), f32[256,256]{0,1:T(8,128)}) %all-reduce.6.cloned.1.call-update) | async-done | bytes 262160 | tf_op jit(solution)/shard_map/psum | solution.py:25
  735.6 1.1 copy.14
  736.7 1.0 fusion.10
  737.7 11.7 %cholesky.50 = f32[128,128]{1,0:T(8,128)S(1)} custom-call(f32[128,128]{1,0:T(8,128)S(1)} %cholesky.118), custom_call_target="Cholesky" | custom-call | tf_op jit(solution)/shard_map/jit(cholesky)/cholesky | solution.py:26
  749.4 9.8 %custom-call.15 = f32[1,128,128]{1,2,0:T(8,128)S(1)} custom-call(f32[1,128,128]{2,1,0:T(8,128)S(1)} %get-tuple-element.26), custom_call_target="InvertDiagBlocksLowerTriangular" | custom-call | tf_op jit(solution)/shard_map/jit(cholesky)/cholesky | solution.py:26
  759.3 0.2 constant_dynamic-update-slice_fusion.1
  759.5 0.3 convolution_subtract_fusion.1
  759.8 11.7 %cholesky.105 = f32[128,128]{1,0:T(8,128)S(1)} custom-call(f32[128,128]{1,0:T(8,128)S(1)} %convolution_subtract_fusion.1), custom_call_target="Cholesky" | custom-call | tf_op jit(solution)/shard_map/jit(cholesky)/cholesky | solution.py:26
  771.5 0.7 compare_reduce_fusion
  773.5 0.1 triangular_solve.57
  773.6 4.1 while.1
  773.8 0.6 fusion.31
  774.3 1.3 bitcast_dynamic-update-slice_fusion.2
  775.7 0.6 fusion.31
  776.3 1.3 bitcast_dynamic-update-slice_fusion.2
  777.7 19.7 %custom-call.16 = f32[2,128,128]{1,2,0:T(8,128)S(1)} custom-call(f32[2,128,128]{2,1,0:T(8,128)S(1)} %get-tuple-element.12), custom_call_target="InvertDiagBlocksLowerTriangular" | custom-call | tf_op jit(solution)/shard_map/jit(_solve_triangular)/triangular_solve | solution.py:27
  797.3 1.0 fusion.18
  798.3 1.0 convolution_subtract_fusion.2
  799.3 0.2 convolution_convert_fusion
  799.5 0.6 maximum_bitcast_fusion
  800.2 0.0 all-gather.5.cloned.1.call-update
  800.2 0.0 copy-done.1
  800.2 0.1 dynamic_slice.3
  800.3 0.1 iota_compare_fusion.3
  800.4 75.3 %all-gather.5.cloned.1.call-done = bf16[5120,256]{1,0:T(8,128)(2,1)} async-done(((bf16[80,256]{1,0:T(8,128)(2,1)}), bf16[5120,256]{1,0:T(8,128)(2,1)}) %all-gather.5.cloned.1.call-update) | async-done | bytes 2621456 | tf_op jit(solution)/shard_map/all_gather | solution.py:30
  875.7 4.9 fusion.7
  880.6 1.0 copy.16
  (9 shorter events, 0.1 us)
Async XLA Ops:
  6.5 353.9 %copy-start = (bf16[2,256,256]{2,1,0:T(8,128)(2,1)S(1)}, bf16[2,256,256]{2,1,0:T(8,128)(2,1)}, u32[]{:S(2)}) copy-start(bf16[2,256,256]{2,1,0:T(8,128)(2,1)} %param.8) | copy-start | bytes 786436
  6.5 114.8 %all-gather.3.cloned.1.call-start = ((), (), s32[]{:S(2)}) async-start(), calls=%async_computation.2 | async-start | bytes 17039360 | tf_op jit(solution)/shard_map/all_gather | solution.py:13
  7.3 497.5 %reduce-scatter.2.cloned.1.call-start = ((), (), s32[]{:S(2)}) async-start(), calls=%async_computation.3 | async-start | bytes 5324800 | tf_op jit(solution)/shard_map/reduce_scatter | solution.py:18
  366.7 433.5 %copy-start.1 = (s32[8]{0:T(128)S(1)}, s32[8]{0:T(128)}, u32[]{:S(2)}) copy-start(s32[8]{0:T(128)} %param.9) | copy-start | bytes 100
  366.8 187.5 %all-reduce.4.cloned.1.call-start = ((), (), s32[]{:S(2)}) async-start(), calls=%async_computation.4 | async-start | bytes 163840 | tf_op jit(solution)/shard_map/psum | solution.py:24
  504.8 230.8 %all-reduce.6.cloned.1.call-start = ((), (), s32[]{:S(2)}) async-start(), calls=%async_computation.5 | async-start | bytes 524288 | tf_op jit(solution)/shard_map/psum | solution.py:25
  556.4 319.3 %all-gather.5.cloned.1.call-start = ((), (), s32[]{:S(2)}) async-start(), calls=%async_computation.6 | async-start | bytes 2662400 | tf_op jit(solution)/shard_map/all_gather | solution.py:30
Sparse Core Ops, SparseCore 0:
  10.0 111.3 all-gather.2
  366.9 137.8 reduce-scatter.1
  507.2 46.9 all-reduce.3
  557.6 177.9 all-reduce.5
  800.3 75.3 all-gather.4
where the time goes:
time: 889 us; the launch traced here: 888 us
  waiting for transfers between devices  557 us (63%)
  blocking collectives  191 us (21%)
  other arithmetic  55.4 us (6%)
  local copies, waits for them, and re-layouts  41.8 us (5%)
  matrix products  28.4 us (3%)
  between operations  14.5 us (2%)
    all_to_all x1, blocking collectives, per_device(): lax.all_to_all(residual_rows, 'row', split_axis=2, concat_axis=1, tiled=T...  191 us
    psum x1, waiting for transfers between devices, per_device(): lax.psum(jnp.dot(row_sketch.T, row_sketch, precision=lax.Precision.HIGHES...  179 us
    reduce_scatter x1, waiting for transfers between devices, per_device(): lax.psum_scatter(jnp.einsum('lrc,lcs->rs', residual, sketch_map, preferre...  138 us
    all_gather x1, waiting for transfers between devices, per_device(): lax.all_gather(basis, 'row', axis=1, tiled=True)  114 us
    all_gather x1, waiting for transfers between devices, per_device(): ortho = lax.all_gather(ortho_rows, 'row', axis=0, tiled=True)  75.3 us
    psum x1, waiting for transfers between devices, per_device(): row_sketch = lax.psum(row_sketch, 'layer')  49.4 us
    another operation x6, other arithmetic, per_device(): factor = jnp.linalg.cholesky(gram)  34 us
    another operation x3, other arithmetic, per_device(): jax.scipy.linalg.solve_triangular(factor, row_sketch.T, lower=True)  19.7 us
  transfers between devices with their start and end apart: 5, of which 5 were waited for; matrix products, arithmetic and copies ran while one was open for 0% of the time, Pallas kernels for 0%

commit v1 on v0

v1 whole, which is shorter than its diff:
```python
import functools

import jax
import jax.numpy as jnp
from jax import lax
from jax.experimental import pallas as pl
from jax.experimental.pallas import tpu as pltpu
from jax.sharding import Mesh
from jax.sharding import PartitionSpec as P

ROW = ("z", "y", "c")
BLK = 64


def cut_kernel(w_ref, o_ref):
    groups, cols = o_ref.shape[0], o_ref.shape[3]
    for g in range(groups):
        o_ref[g, 0] = w_ref[0, :, g * cols : (g + 1) * cols]


def cut_by_owner(weights, groups, planes):
    lay, rows, width = weights.shape
    cols = width // (groups * planes)
    return pl.pallas_call(
        cut_kernel,
        grid=(lay, planes),
        in_specs=[pl.BlockSpec((1, rows, groups * cols), lambda l, z: (l, 0, z))],
        out_specs=pl.BlockSpec((groups, 1, rows, cols), lambda l, z: (0, l, 0, z)),
        out_shape=jax.ShapeDtypeStruct((groups, lay, rows, planes * cols), weights.dtype),
        name="cut_by_owner",
    )(weights)


def residual_kernel(w_ref, c_ref, b_ref, m_ref, r_ref, s_ref):
    groups, _, rows, cols = w_ref.shape
    low = jnp.dot(
        c_ref[:, 0].reshape(groups * rows, -1), b_ref[0], preferred_element_type=jnp.float32
    )
    res = w_ref[:, 0].reshape(groups * rows, cols).astype(jnp.float32) - low
    res = res.astype(jnp.bfloat16)
    r_ref[:, 0] = res.reshape(groups, rows, cols)
    part = jnp.dot(res, m_ref[0, 0], preferred_element_type=jnp.float32)
    first = (pl.program_id(0) == 0) & (pl.program_id(1) == 0)

    @pl.when(first)
    def _():
        s_ref[...] = part

    @pl.when(jnp.logical_not(first))
    def _():
        s_ref[...] += part


def residual_and_sketch(w, coeffs, basis, maps):
    groups, lay, rows, width = w.shape
    planes, rank, cols = basis.shape
    sw = maps.shape[3]
    return pl.pallas_call(
        residual_kernel,
        grid=(lay, planes),
        in_specs=[
            pl.BlockSpec((groups, 1, rows, cols), lambda l, z: (0, l, 0, z)),
            pl.BlockSpec((groups, 1, rows, rank), lambda l, z: (0, l, 0, 0)),
            pl.BlockSpec((1, rank, cols), lambda l, z: (z, 0, 0)),
            pl.BlockSpec((1, 1, cols, sw), lambda l, z: (z, l, 0, 0)),
        ],
        out_specs=[
            pl.BlockSpec((groups, 1, rows, cols), lambda l, z: (0, l, 0, z)),
            pl.BlockSpec((groups * rows, sw), lambda l, z: (0, 0)),
        ],
        out_shape=[
            jax.ShapeDtypeStruct(w.shape, jnp.bfloat16),
            jax.ShapeDtypeStruct((groups * rows, sw), jnp.float32),
        ],
        name="residual_and_sketch",
    )(w, coeffs, basis, maps)


def project_kernel(s_ref, r_ref, o_ref, hi_ref, lo_ref):
    groups, _, rows, cols = r_ref.shape

    @pl.when((pl.program_id(0) == 0) & (pl.program_id(1) == 0))
    def _():
        st = s_ref[...].T
        hi = st.astype(jnp.bfloat16)
        hi_ref[...] = hi
        lo_ref[...] = (st - hi.astype(jnp.float32)).astype(jnp.bfloat16)

    res = r_ref[:, 0].reshape(groups * rows, cols)
    o_ref[0, 0] = jnp.dot(hi_ref[...], res, preferred_element_type=jnp.float32) + jnp.dot(
        lo_ref[...], res, preferred_element_type=jnp.float32
    )


def project(sketch, residual, planes):
    groups, lay, rows, width = residual.shape
    cols = width // planes
    sw = sketch.shape[1]
    return pl.pallas_call(
        project_kernel,
        grid=(lay, planes),
        in_specs=[
            pl.BlockSpec((groups * rows, sw), lambda l, z: (0, 0)),
            pl.BlockSpec((groups, 1, rows, cols), lambda l, z: (0, l, 0, z)),
        ],
        out_specs=pl.BlockSpec((1, 1, sw, cols), lambda l, z: (z, l, 0, 0)),
        out_shape=jax.ShapeDtypeStruct((planes, lay, sw, cols), jnp.float32),
        scratch_shapes=[
            pltpu.VMEM((sw, groups * rows), jnp.bfloat16),
            pltpu.VMEM((sw, groups * rows), jnp.bfloat16),
        ],
        name="project",
    )(sketch, residual)


def dot32(a, b, dims=((1,), (0,))):
    return lax.dot_general(
        a, b, (dims, ((), ())), precision=lax.Precision.HIGHEST, preferred_element_type=jnp.float32
    )


def factor_block(a):
    n = a.shape[0]
    row = lax.broadcasted_iota(jnp.int32, (n, n), 0)
    col = lax.broadcasted_iota(jnp.int32, (n, n), 1)
    both = jnp.concatenate([a, jnp.where(row == col, 1.0, 0.0)], axis=1)
    below = lax.broadcasted_iota(jnp.int32, (n, 2 * n), 0)
    done = []
    for j in range(n):
        pivot = lax.rsqrt(both[j : j + 1, j : j + 1])
        line = both[j : j + 1, :] * pivot
        mult = both[:, j : j + 1] * pivot
        done.append(line)
        both = both - jnp.where(below > j, mult * line, 0.0)
    return jnp.concatenate(done, axis=0)[:, n:]


def inverse_factor_kernel(g_ref, o_ref, a_ref):
    n = g_ref.shape[0]
    a_ref[...] = g_ref[...]
    o_ref[...] = jnp.zeros_like(o_ref)
    for k in range(0, n, BLK):
        e = k + BLK
        inv = factor_block(a_ref[k:e, k:e])
        o_ref[k:e, k:e] = inv
        if k:
            o_ref[k:e, :k] = dot32(inv, o_ref[k:e, :k])
        if e < n:
            panel = dot32(a_ref[e:, k:e], inv, ((1,), (1,)))
            a_ref[e:, e:] -= dot32(panel, panel, ((1,), (1,)))
            o_ref[e:, :e] -= dot32(panel, o_ref[k:e, :e])


def inverse_factor(gram):
    return pl.pallas_call(
        inverse_factor_kernel,
        out_shape=jax.ShapeDtypeStruct(gram.shape, jnp.float32),
        scratch_shapes=[pltpu.VMEM(gram.shape, jnp.float32)],
        name="inverse_factor",
    )(gram)


def finish_kernel(ranks_ref, inv_ref, p_ref, o_ref):
    l = pl.program_id(0)
    out = dot32(inv_ref[...], p_ref[0])
    kept = lax.broadcasted_iota(jnp.int32, out.shape, 0) < ranks_ref[l]
    o_ref[0] = jnp.where(kept, out, 0.0)


def finish(ranks, inv, proj):
    lay, sw, cols = proj.shape
    return pl.pallas_call(
        finish_kernel,
        grid=(lay,),
        in_specs=[
            pl.BlockSpec(memory_space=pltpu.SMEM),
            pl.BlockSpec((sw, sw), lambda l: (0, 0)),
            pl.BlockSpec((1, sw, cols), lambda l: (l, 0, 0)),
        ],
        out_specs=pl.BlockSpec((1, sw, cols), lambda l: (l, 0, 0)),
        out_shape=jax.ShapeDtypeStruct(proj.shape, jnp.float32),
        name="finish",
    )(ranks, inv, proj)


def sum_over(x, axis, size):
    parts = [x] + [
        lax.ppermute(x, axis, [(i, (i + k) % size) for i in range(size)]) for k in range(1, size)
    ]
    return sum(parts[1:], parts[0])


def per_device(planes, groups, lines, weights, coeffs, basis, sketch_map, ranks):
    lay = weights.shape[0]
    sw = sketch_map.shape[2]
    cut = cut_by_owner(weights, groups, planes)
    res_in = lax.all_to_all(cut, ("y", "c"), 0, 0, tiled=True)
    all_coeffs = lax.all_gather(coeffs, ("y", "c"), axis=0)
    all_basis = lax.all_gather(basis, "z", axis=0)
    all_maps = lax.all_gather(sketch_map, "z", axis=0)
    residual, part = residual_and_sketch(res_in, all_coeffs, all_basis, all_maps)
    rows = part.shape[0] // groups
    part = lax.all_to_all(part.reshape(groups, rows, sw), ("y", "c"), 0, 0, tiled=True)
    own = sum_over(part.sum(0), "x", lines)
    sketch = lax.all_to_all(
        jnp.broadcast_to(own[None], (groups, rows, sw)), ("y", "c"), 0, 0, tiled=True
    ).reshape(groups * rows, sw)
    proj = lax.psum_scatter(project(sketch, residual, planes), "z", scatter_dimension=0)
    gram = dot32(sketch, sketch, ((0,), (0,)))
    gram = lax.all_to_all(gram.reshape(planes, sw // planes, sw), "z", 0, 0, tiled=True).sum(0)
    gram = lax.all_to_all(
        jnp.broadcast_to(gram[None], (planes, sw // planes, sw)), "z", 0, 0, tiled=True
    ).reshape(sw, sw)
    inv = inverse_factor(gram)
    ranks_here = lax.dynamic_slice_in_dim(ranks, lax.axis_index("x") * lay, lay)
    return finish(ranks_here, inv, proj)


def solution(mesh):
    wide, lines = mesh.devices.shape
    groups = 8
    planes = wide // groups
    fine = Mesh(mesh.devices.reshape(planes, groups // 2, 2, lines), ROW + ("x",))
    in_specs = (
        P("x", ROW, None),
        P("x", ROW, None),
        P(None, ROW),
        P("x", ROW, None),
        P(),
    )
    return jax.shard_map(
        functools.partial(per_device, planes, groups, lines),
        mesh=fine,
        in_specs=in_specs,
        out_specs=P("x", None, ROW),
        check_vma=False,
    )
```

time: 889 us -> 272 us (0.31)
  waiting for transfers between devices: 557 us -> 117 us
  blocking collectives: 191 us -> 50 us
  Pallas kernels: 0 us -> 69 us
  other arithmetic: 55.4 us -> 0.09 us
  local copies, waits for them, and re-layouts: 41.8 us -> 2.38 us
  matrix products: 28.4 us -> 0.8 us
  starting transfers between devices: 0.34 us -> 16.1 us
    psum x2 -> x0, waiting for transfers between devices: 228 us -> none  [the longest x1 179 us: per_device(): lax.psum(jnp.dot(row_sketch.T, row_sketch, precision=lax.Precision.HIGHES...]
    all_to_all x1 -> x3, blocking collectives: 191 us -> 50 us  [the longest x1 19.6 us: per_device(): lax.all_to_all(part.reshape(groups, rows, sw), ('y', 'c'), 0, 0, tiled=True)]
    reduce_scatter x1, waiting for transfers between devices: 138 us -> 1.78 us  [per_device(): lax.psum_scatter(project(sketch, residual, planes), 'z', scatter_dimensio...]
    all_gather x2 -> x3, waiting for transfers between devices: 189 us -> 98.3 us  [the longest x1 41.6 us: per_device(): all_maps = lax.all_gather(sketch_map, 'z', axis=0)]
    pallas_call x0 -> x5, Pallas kernels: none -> 69 us  [the longest x1 25.4 us: inverse_factor(): pl.pallas_call(inverse_factor_kernel, out_shape=jax.ShapeDtypeStruct(gram...]
    another operation x9 -> x0, other arithmetic: 53.7 us -> none  [the longest x6 34 us: per_device(): factor = jnp.linalg.cholesky(gram)]
    dot_general x4 -> x1, matrix products: 25.8 us -> 0.8 us  [dot32(): lax.dot_general(a, b, (dims, ((), ())), precision=lax.Precision.HIGHEST,...]
    convert_element_type x1 -> x0, local copies, waits for them, and re-layouts: 18 us -> none  [per_device(): residual_rows = (weights.astype(jnp.float32) - lowrank).astype(jnp.bfloat16)]
  transfers between devices with their start and end apart: 5 -> 9, of which waited for: 5 -> 7; matrix products, arithmetic and copies ran while one was open for 0% -> 1% of each run, Pallas kernels for 0% -> 13%
where the time goes in v1:
time: 272 us; the launch traced here: 269 us
  waiting for transfers between devices  117 us (43%)
  Pallas kernels  69 us (25%)
  blocking collectives  50 us (18%)
  starting transfers between devices  16.1 us (6%)
  between operations  13.2 us (5%)
    all_gather x1, waiting for transfers between devices, per_device(): all_maps = lax.all_gather(sketch_map, 'z', axis=0)  41.6 us
    all_gather x1, waiting for transfers between devices, per_device(): all_basis = lax.all_gather(basis, 'z', axis=0)  39.7 us
    pallas_call x1, Pallas kernels, inverse_factor(): pl.pallas_call(inverse_factor_kernel, out_shape=jax.ShapeDtypeStruct(gram...  25.4 us
    all_to_all x1, blocking collectives, per_device(): lax.all_to_all(part.reshape(groups, rows, sw), ('y', 'c'), 0, 0, tiled=True)  19.6 us
    all_gather x1, waiting for transfers between devices, per_device(): all_coeffs = lax.all_gather(coeffs, ('y', 'c'), axis=0)  17 us
    pallas_call x1, Pallas kernels, residual_and_sketch(): pl.pallas_call(residual_kernel, grid=(lay, planes), in_specs=[pl.BlockSpe...  16.8 us
    all_to_all x1, blocking collectives, per_device(): lax.all_to_all(jnp.broadcast_to(own[None], (groups, rows, sw)), ('y', 'c'...  15.6 us
    all_to_all x1, blocking collectives, per_device(): lax.all_to_all(gram.reshape(planes, sw // planes, sw), 'z', 0, 0, tiled=T...  14.7 us
  transfers between devices with their start and end apart: 9, of which 7 were waited for; matrix products, arithmetic and copies ran while one was open for 1% of the time, Pallas kernels for 13%

profile of v1, /device:TPU:1, one launch (start us, length us, event | category | flops | bytes accessed | tf_op | source)
XLA Modules:
  0.0 268.9 jit_solution(17246498432795389792)
XLA Ops:
  6.5 0.0 all-gather.7.cloned.1.call-start
  6.5 0.7 all-gather.7.cloned.1.call-update
  7.3 0.0 all-gather.9.cloned.1.call-start
  7.3 0.7 all-gather.9.cloned.1.call-update
  8.0 10.7 %cut_by_owner.1 = bf16[8,2,80,2048]{3,2,1,0:T(8,128)(2,1)} custom-call(bf16[2,80,16384]{2,1,0:T(8,128)(2,1)} %w_ref.1), custom_call_target="tpu_custom_call" | custom-call | tf_op jit(solution)/shard_map/cut_by_owner/pallas_call | solution.py:24
  18.7 7.8 %all-to-all-start = ((bf16[8,2,80,2048]{3,2,1,0:T(8,128)(2,1)}), bf16[8,2,80,2048]{3,2,1,0:T(8,128)(2,1)}, u32[]{:S(2)}, u32[]{:S(2)}) async-start(bf16[8,2,80,2048]{3,2,1,0:T(8,128)(2,1)} %cut_by_owner.1), calls=%async_computation | async-start | bytes 10485760 | tf_op jit(solution)/shard_map/all_to_all | solution.py:197
  26.5 0.0 all-gather.11.cloned.1.call-start
  26.5 0.7 all-gather.11.cloned.1.call-update
  27.2 0.0 reduce-scatter.2.cloned.1.call-start
  27.2 17.0 %all-gather.7.cloned.1.call-done = bf16[16,80,512]{2,1,0:T(8,128)(2,1)} async-done(((bf16[2,80,512]{2,1,0:T(8,128)(2,1)}), bf16[16,80,512]{2,1,0:T(8,128)(2,1)}) %all-gather.7.cloned.1.call-update) | async-done | bytes 1310736 | tf_op jit(solution)/shard_map/all_gather | solution.py:198
  44.2 39.7 %all-gather.9.cloned.1.call-done = bf16[4096,256]{1,0:T(8,128)(2,1)} async-done(((bf16[512,256]{1,0:T(8,128)(2,1)}), bf16[4096,256]{1,0:T(8,128)(2,1)}) %all-gather.9.cloned.1.call-update) | async-done | bytes 2097168 | tf_op jit(solution)/shard_map/all_gather | solution.py:199
  83.9 41.6 %all-gather.11.cloned.1.call-done = bf16[16,256,256]{2,1,0:T(8,128)(2,1)} async-done(((bf16[2,256,256]{2,1,0:T(8,128)(2,1)}), bf16[16,256,256]{2,1,0:T(8,128)(2,1)}) %all-gather.11.cloned.1.call-update) | async-done | bytes 2097168 | tf_op jit(solution)/shard_map/all_gather | solution.py:200
  125.5 0.0 all-to-all-done.w_ref
  125.5 16.8 %residual_and_sketch.1 = (bf16[8,2,80,2048]{3,2,1,0:T(8,128)(2,1)}, f32[640,256]{1,0:T(8,128)}) custom-call(bf16[8,2,80,2048]{3,2,1,0:T(8,128)(2,1)} %all-to-all-done.w_ref, bf16[8,2,80,512]{3,2,1,0:T(8,128)(2,1)} %bitcast.20, bf16[8,512,256]{2,1,0:T(8,128)(2,1)} %bitcast.18, bf16[8,2,256,256]{3,2,1,0:T(8,128)(2,1)} %bitcast.19), custom_call_target="tpu_custom_call" | custom-call | tf_op jit(solution)/shard_map/residual_and_sketch/pallas_call | solution.py:58
  142.3 19.6 %all_to_all.25 = f32[8,80,256]{2,1,0:T(8,128)S(1)} all-to-all(f32[8,80,256]{2,1,0:T(8,128)} %bitcast.22), channel_id=1, replica_groups=mesh['z'=8,'y'=4,'c'=2,'x'=4] {'y','c'}, dimensions={0} | all-to-all | bytes 1310720 | tf_op jit(solution)/shard_map/all_to_all | solution.py:203
  162.0 1.3 collective-permute-start
  163.3 2.4 collective-permute-start.1
  165.7 1.2 collective-permute-start.2
  166.8 0.0 collective-permute-done
  166.9 1.9 collective-permute-done.1
  168.8 1.2 collective-permute-done.2
  170.0 15.6 %all_to_all.26 = f32[8,80,256]{2,1,0:T(8,128)} all-to-all(f32[8,80,256]{2,1,0:T(8,128)S(1)} %broadcast_in_dim.4), channel_id=1, replica_groups=mesh['z'=8,'y'=4,'c'=2,'x'=4] {'y','c'}, dimensions={0} | all-to-all | bytes 1310720 | tf_op jit(solution)/shard_map/all_to_all | solution.py:205
  185.6 0.0 copy-start
  185.6 13.5 %project.1 = f32[8,2,256,256]{3,2,1,0:T(8,128)} custom-call(f32[640,256]{1,0:T(8,128)} %bitcast.14, bf16[8,2,80,2048]{3,2,1,0:T(8,128)(2,1)} %get-tuple-element.8.r_ref), custom_call_target="tpu_custom_call" | custom-call | tf_op jit(solution)/shard_map/project/pallas_call | solution.py:99
  199.2 0.0 copy-start.2
  199.2 0.0 reduce-scatter.2.cloned.1.call-update
  199.2 0.0 copy-done
  199.2 0.2 copy.8
  199.4 0.8 fusion
  200.2 14.7 %all_to_all.27 = f32[8,32,256]{2,1,0:T(8,128)S(1)} all-to-all(f32[8,32,256]{2,1,0:T(8,128)S(1)} %fusion), channel_id=1, replica_groups=mesh['z'=8,'y'=4,'c'=2,'x'=4] {'z'}, dimensions={0} | all-to-all | bytes 524288 | tf_op jit(solution)/shard_map/all_to_all | solution.py:210
  215.0 0.7 broadcast_in_dim.5
  215.7 3.4 %all-to-all-start.4 = ((f32[8,32,256]{2,1,0:T(8,128)}), f32[8,32,256]{2,1,0:T(8,128)S(1)}, u32[]{:S(2)}, u32[]{:S(2)}) async-start(f32[8,32,256]{2,1,0:T(8,128)} %broadcast_in_dim.5), calls=%async_computation.4 | async-start | bytes 524288 | tf_op jit(solution)/shard_map/all_to_all | solution.py:211
  219.2 0.0 copy-done.2
  219.2 0.7 dynamic_slice.3.ranks_ref
  219.8 12.1 %all-to-all-done.4 = f32[8,32,256]{2,1,0:T(8,128)S(1)} async-done(((f32[8,32,256]{2,1,0:T(8,128)}), f32[8,32,256]{2,1,0:T(8,128)S(1)}, u32[]{:S(2)}, u32[]{:S(2)}) %all-to-all-start.4) | async-done | bytes 262176 | tf_op jit(solution)/shard_map/all_to_all | solution.py:211
  231.9 0.0 copy-start.1
  231.9 0.7 copy-done.1
  232.6 25.4 %inverse_factor.1.inv_ref = f32[256,256]{1,0:T(8,128)} custom-call(f32[256,256]{1,0:T(8,128)} %bitcast.21), custom_call_target="tpu_custom_call" | custom-call | tf_op jit(solution)/shard_map/inverse_factor/pallas_call | solution.py:155
  258.0 1.8 reduce-scatter.2.cloned.1.call-done
  259.8 2.5 finish.1
  (4 shorter events, 0.1 us)
Async XLA Ops:
  6.5 37.7 %all-gather.7.cloned.1.call-start = ((), (), s32[]{:S(2)}) async-start(), calls=%async_computation.7 | async-start | bytes 1474560 | tf_op jit(solution)/shard_map/all_gather | solution.py:198
  7.3 76.6 %all-gather.9.cloned.1.call-start = ((), (), s32[]{:S(2)}) async-start(), calls=%async_computation.8 | async-start | bytes 2359296 | tf_op jit(solution)/shard_map/all_gather | solution.py:199
  18.7 106.9 %all-to-all-start = ((bf16[8,2,80,2048]{3,2,1,0:T(8,128)(2,1)}), bf16[8,2,80,2048]{3,2,1,0:T(8,128)(2,1)}, u32[]{:S(2)}, u32[]{:S(2)}) async-start(bf16[8,2,80,2048]{3,2,1,0:T(8,128)(2,1)} %cut_by_owner.1), calls=%async_computation | async-start | bytes 10485760 | tf_op jit(solution)/shard_map/all_to_all | solution.py:197
  26.5 99.1 %all-gather.11.cloned.1.call-start = ((), (), s32[]{:S(2)}) async-start(), calls=%async_computation.9 | async-start | bytes 2359296 | tf_op jit(solution)/shard_map/all_gather | solution.py:200
  27.2 232.6 %reduce-scatter.2.cloned.1.call-start = ((), (), s32[]{:S(2)}) async-start(), calls=%async_computation.6 | async-start | bytes 4718592 | tf_op jit(solution)/shard_map/reduce_scatter | solution.py:208
  162.0 4.8 %collective-permute-start = (f32[80,256]{1,0:T(8,128)S(1)}, f32[80,256]{1,0:T(8,128)S(1)}, u32[]{:S(2)}, u32[]{:S(2)}) collective-permute-start(f32[80,256]{1,0:T(8,128)S(1)} %reduce_sum.18), channel_id=1, source_target_pairs={{0,1},{1,2},{2,3},{3,0},{4,5},{5,6},{6,7},{7,4},{8,9},{9,10},{10,1... | collective-permute-start | bytes 245768 | tf_op jit(solution)/shard_map/ppermute | solution.py:188
  163.3 5.5 %collective-permute-start.1 = (f32[80,256]{1,0:T(8,128)S(1)}, f32[80,256]{1,0:T(8,128)S(1)}, u32[]{:S(2)}, u32[]{:S(2)}) collective-permute-start(f32[80,256]{1,0:T(8,128)S(1)} %reduce_sum.18), channel_id=1, source_target_pairs={{0,2},{1,3},{2,0},{3,1},{4,6},{5,7},{6,4},{7,5},{8,10},{9,11},{10,... | collective-permute-start | bytes 245768 | tf_op jit(solution)/shard_map/ppermute | solution.py:188
  165.7 4.3 %collective-permute-start.2 = (f32[80,256]{1,0:T(8,128)S(1)}, f32[80,256]{1,0:T(8,128)S(1)}, u32[]{:S(2)}, u32[]{:S(2)}) collective-permute-start(f32[80,256]{1,0:T(8,128)S(1)} %reduce_sum.18), channel_id=1, source_target_pairs={{0,3},{1,0},{2,1},{3,2},{4,7},{5,4},{6,5},{7,6},{8,11},{9,8},{10,9... | collective-permute-start | bytes 245768 | tf_op jit(solution)/shard_map/ppermute | solution.py:188
  185.6 13.5 %copy-start = (f32[8,80,256]{2,1,0:T(8,128)S(1)}, f32[8,80,256]{2,1,0:T(8,128)}, u32[]{:S(2)}) copy-start(f32[8,80,256]{2,1,0:T(8,128)} %all_to_all.26) | copy-start | bytes 1966084
  199.2 20.0 %copy-start.2 = (s32[8]{0:T(128)S(1)}, s32[8]{0:T(128)}, u32[]{:S(2)}) copy-start(s32[8]{0:T(128)} %param.9) | copy-start | bytes 100
  215.7 16.2 %all-to-all-start.4 = ((f32[8,32,256]{2,1,0:T(8,128)}), f32[8,32,256]{2,1,0:T(8,128)S(1)}, u32[]{:S(2)}, u32[]{:S(2)}) async-start(f32[8,32,256]{2,1,0:T(8,128)} %broadcast_in_dim.5), calls=%async_computation.4 | async-start | bytes 524288 | tf_op jit(solution)/shard_map/all_to_all | solution.py:211
  231.9 0.7 copy-start.1
Sparse Core Ops, SparseCore 0:
  9.2 34.9 all-gather.6
  46.0 37.8 all-gather.8
  85.7 39.8 all-gather.10
  199.3 60.4 reduce-scatter.1

commit v2 on v1

v2 whole, which is shorter than its diff:
```python
import functools

import jax
import jax.numpy as jnp
from jax import lax
from jax.experimental import pallas as pl
from jax.experimental.pallas import tpu as pltpu
from jax.sharding import Mesh
from jax.sharding import PartitionSpec as P

ROW = ("z", "y", "c")
CORES = 2
BLK = 128
STEP = 4
VMEM = 48 * 1024 * 1024
PARAMS = pltpu.CompilerParams(vmem_limit_bytes=VMEM)
SCALARS = pl.BlockSpec(memory_space=pltpu.SMEM)


def cut_kernel(cols, w_ref, o_ref):
    groups, wide = o_ref.shape[0], o_ref.shape[3]
    for z in range(wide // cols):
        for g in range(groups):
            at = (z * groups + g) * cols
            o_ref[g, :, :, z * cols : (z + 1) * cols] = w_ref[:, :, at : at + cols]


def cut_by_owner(weights, groups, planes):
    lay, rows, width = weights.shape
    cols = width // (groups * planes)
    step = 2
    return pl.pallas_call(
        functools.partial(cut_kernel, cols),
        grid=(planes // step,),
        in_specs=[pl.BlockSpec((lay, rows, groups * cols * step), lambda z: (0, 0, z))],
        out_specs=pl.BlockSpec((groups, lay, rows, cols * step), lambda z: (0, 0, 0, z)),
        out_shape=jax.ShapeDtypeStruct((groups, lay, rows, planes * cols), weights.dtype),
        compiler_params=PARAMS,
        name="cut_by_owner",
    )(weights)


def group_at(pos_ref, k, groups, sign):
    lines = groups // CORES
    y = lax.rem(pos_ref[0] + sign * (k // CORES) + lines, lines)
    c = lax.rem(pos_ref[1] + k % CORES, CORES)
    return y * CORES + c


def residual_kernel(pos_ref, w_ref, c_ref, d_ref, b_ref, m_ref, r_ref, *rest):
    groups, _, rows, _ = w_ref.shape
    s_refs, (acc_ref, all_ref) = rest[:groups], rest[groups:]
    step, _, cols = b_ref.shape
    layer, plane = pl.program_id(0), pl.program_id(1)
    tall = groups * rows

    @pl.when((layer == 0) & (plane == 0))
    def _():
        acc_ref[...] = jnp.zeros_like(acc_ref)

    @pl.when(plane == 0)
    def _():
        for k in range(groups):
            at = pl.multiple_of(group_at(pos_ref, k, groups, -1) * rows, 16)
            all_ref[pl.ds(at, rows)] = (c_ref, d_ref)[k % CORES][k // CORES, 0]

    total = None
    for i in range(step):
        here = slice(i * cols, (i + 1) * cols)
        low = jnp.dot(all_ref[...], b_ref[i], preferred_element_type=jnp.float32)
        w = w_ref[:, 0, :, here].reshape(tall, cols).astype(jnp.float32)
        res = (w - low).astype(jnp.bfloat16)
        r_ref[:, 0, :, here] = res.reshape(groups, rows, cols)
        part = jnp.dot(res, m_ref[i], preferred_element_type=jnp.float32)
        total = part if total is None else total + part
    acc_ref[...] += total

    @pl.when((layer == pl.num_programs(0) - 1) & (plane == pl.num_programs(1) - 1))
    def _():
        for k in range(groups):
            at = pl.multiple_of(group_at(pos_ref, k, groups, 1) * rows, 16)
            s_refs[k][...] = acc_ref[pl.ds(at, rows)]


def residual_and_sketch(pos, w, coeffs, others, maps_basis, rank):
    groups, lay, rows, width = w.shape
    planes, _, sw = maps_basis.shape
    cols = width // planes
    mine = pl.BlockSpec((groups // CORES, 1, rows, rank), lambda l, z: (0, l, 0, 0))
    return pl.pallas_call(
        residual_kernel,
        grid=(lay, planes // STEP),
        in_specs=[
            SCALARS,
            pl.BlockSpec((groups, 1, rows, cols * STEP), lambda l, z: (0, l, 0, z)),
            mine,
            mine,
            pl.BlockSpec((STEP, rank, cols), lambda l, z: (z, 1, 0)),
            pl.BlockSpec((STEP, cols, sw), lambda l, z: (z, l, 0)),
        ],
        out_specs=[pl.BlockSpec((groups, 1, rows, cols * STEP), lambda l, z: (0, l, 0, z))]
        + [pl.BlockSpec((rows, sw), lambda l, z: (0, 0))] * groups,
        out_shape=[jax.ShapeDtypeStruct(w.shape, jnp.bfloat16)]
        + [jax.ShapeDtypeStruct((rows, sw), jnp.float32)] * groups,
        scratch_shapes=[
            pltpu.VMEM((groups * rows, sw), jnp.float32),
            pltpu.VMEM((groups * rows, rank), jnp.bfloat16),
        ],
        compiler_params=PARAMS,
        name="residual_and_sketch",
    )(pos, w, coeffs, others, maps_basis, maps_basis)


def gram_kernel(pos_ref, *refs):
    both_ref, g_ref, s_ref = refs[-3:]
    parts = refs[:-3]
    groups = len(parts)
    rows, sw = parts[0].shape
    for k in range(groups):
        at = pl.multiple_of(group_at(pos_ref, k, groups, -1) * rows, 16)
        s_ref[pl.ds(at, rows)] = parts[k][...]
    st = s_ref[...].T
    g_ref[...] = dot32(st, s_ref[...])
    high = st.astype(jnp.bfloat16)
    both_ref[:sw] = high
    both_ref[sw:] = (st - high.astype(jnp.float32)).astype(jnp.bfloat16)


def stack_and_gram(pos, parts):
    rows, sw = parts[0].shape
    tall = rows * len(parts)
    return pl.pallas_call(
        gram_kernel,
        in_specs=[SCALARS] + [pl.BlockSpec((rows, sw), lambda: (0, 0))] * len(parts),
        out_shape=[
            jax.ShapeDtypeStruct((2 * sw, tall), jnp.bfloat16),
            jax.ShapeDtypeStruct((sw, sw), jnp.float32),
        ],
        scratch_shapes=[pltpu.VMEM((tall, sw), jnp.float32)],
        compiler_params=PARAMS,
        name="stack_and_gram",
    )(pos, *parts)


def project_kernel(both_ref, r_ref, o_ref):
    groups, _, rows, wide = r_ref.shape
    step, _, sw, cols = o_ref.shape
    for i in range(step):
        res = r_ref[:, 0, :, i * cols : (i + 1) * cols].reshape(groups * rows, cols)
        out = jnp.dot(both_ref[...], res, preferred_element_type=jnp.float32)
        o_ref[i, 0] = out[:sw] + out[sw:]


def project(both, residual, planes):
    groups, lay, rows, width = residual.shape
    cols = width // planes
    sw = both.shape[0] // 2
    return pl.pallas_call(
        project_kernel,
        grid=(lay, planes // STEP),
        in_specs=[
            pl.BlockSpec(both.shape, lambda l, z: (0, 0)),
            pl.BlockSpec((groups, 1, rows, cols * STEP), lambda l, z: (0, l, 0, z)),
        ],
        out_specs=pl.BlockSpec((STEP, 1, sw, cols), lambda l, z: (z, l, 0, 0)),
        out_shape=jax.ShapeDtypeStruct((planes, lay, sw, cols), jnp.float32),
        compiler_params=PARAMS,
        name="project",
    )(both, residual)


def dot32(a, b, dims=((1,), (0,))):
    return lax.dot_general(
        a, b, (dims, ((), ())), precision=lax.Precision.HIGHEST, preferred_element_type=jnp.float32
    )


def factor_block(a):
    n = a.shape[0]
    row = lax.broadcasted_iota(jnp.int32, (n, n), 0)
    col = lax.broadcasted_iota(jnp.int32, (n, n), 1)
    both = jnp.concatenate([a, jnp.where(row == col, 1.0, 0.0)], axis=1)
    done = []
    for j in range(n):
        r = j % 8
        if j and r == 0:
            both = both[8:]
        pivot = lax.rsqrt(both[r : r + 1, j : j + 1])
        line = both[r : r + 1, :] * pivot
        mult = both[:, j : j + 1] * pivot
        done.append(line)
        if r < 7:
            keep = lax.broadcasted_iota(jnp.int32, (both.shape[0], 1), 0) > r
            mult = jnp.where(keep, mult, 0.0)
        both = both - mult * line
    return jnp.concatenate(done, axis=0)[:, n:]


def inverse_factor_kernel(g_ref, o_ref, a_ref):
    n = g_ref.shape[0]
    a_ref[...] = g_ref[...]
    o_ref[...] = jnp.zeros_like(o_ref)
    for k in range(0, n, BLK):
        e = k + BLK
        inv = factor_block(a_ref[k:e, k:e])
        o_ref[k:e, k:e] = inv
        if k:
            o_ref[k:e, :k] = dot32(inv, o_ref[k:e, :k])
        if e < n:
            panel = dot32(a_ref[e:, k:e], inv, ((1,), (1,)))
            a_ref[e:, e:] -= dot32(panel, panel, ((1,), (1,)))
            o_ref[e:, :e] -= dot32(panel, o_ref[k:e, :e])


def inverse_factor(gram):
    return pl.pallas_call(
        inverse_factor_kernel,
        out_shape=jax.ShapeDtypeStruct(gram.shape, jnp.float32),
        scratch_shapes=[pltpu.VMEM(gram.shape, jnp.float32)],
        compiler_params=PARAMS,
        name="inverse_factor",
    )(gram)


def finish_kernel(ranks_ref, inv_ref, p_ref, o_ref):
    l = pl.program_id(0)
    out = dot32(inv_ref[...], p_ref[0])
    kept = lax.broadcasted_iota(jnp.int32, out.shape, 0) < ranks_ref[l]
    o_ref[0] = jnp.where(kept, out, 0.0)


def finish(ranks, inv, proj):
    lay, sw, cols = proj.shape
    return pl.pallas_call(
        finish_kernel,
        grid=(lay,),
        in_specs=[
            SCALARS,
            pl.BlockSpec((sw, sw), lambda l: (0, 0)),
            pl.BlockSpec((1, sw, cols), lambda l: (l, 0, 0)),
        ],
        out_specs=pl.BlockSpec((1, sw, cols), lambda l: (l, 0, 0)),
        out_shape=jax.ShapeDtypeStruct(proj.shape, jnp.float32),
        compiler_params=PARAMS,
        name="finish",
    )(ranks, inv, proj)


def shift(x, axis, size, k):
    return lax.ppermute(x, axis, [(i, (i + k) % size) for i in range(size)])


def shift_group(x, groups, k):
    lines = groups // CORES
    pairs = [
        (y * CORES + c, (y + k // CORES) % lines * CORES + (c + k) % CORES)
        for y in range(lines)
        for c in range(CORES)
    ]
    return lax.ppermute(x, ("y", "c"), pairs)


def added(parts):
    return sum(parts[1:], parts[0])


def per_device(planes, groups, lines, weights, coeffs, basis, sketch_map, ranks):
    lay, _, _ = weights.shape
    sw = sketch_map.shape[2]
    ys = groups // CORES
    pos = jnp.stack([lax.axis_index("y"), lax.axis_index("c")]).astype(jnp.int32)
    own = jnp.concatenate([sketch_map.reshape(-1, sw), basis], axis=0)
    maps_basis = lax.all_gather(own, "z", axis=0)
    near = jnp.stack([coeffs] + [shift(coeffs, "y", ys, k) for k in range(1, ys)])
    others = shift(near, "c", CORES, 1)
    cut = cut_by_owner(weights, groups, planes)
    res_in = lax.all_to_all(cut, ("y", "c"), 0, 0, tiled=True)
    residual, *parts = residual_and_sketch(pos, res_in, near, others, maps_basis, basis.shape[0])
    mine = added([parts[0]] + [shift_group(parts[k], groups, k) for k in range(1, groups)])
    mine = added([mine] + [shift(mine, "x", lines, k) for k in range(1, lines)])
    rows_of = [mine] + [shift_group(mine, groups, k) for k in range(1, groups)]
    both, gram = stack_and_gram(pos, rows_of)
    proj = lax.psum_scatter(project(both, residual, planes), "z", scatter_dimension=0)
    gram = lax.all_to_all(gram.reshape(planes, sw // planes, sw), "z", 0, 0, tiled=True).sum(0)
    gram = lax.all_to_all(
        jnp.broadcast_to(gram[None], (planes, sw // planes, sw)), "z", 0, 0, tiled=True
    ).reshape(sw, sw)
    inv = inverse_factor(gram)
    ranks_here = lax.dynamic_slice_in_dim(ranks, lax.axis_index("x") * lay, lay)
    return finish(ranks_here, inv, proj)


def solution(mesh):
    wide, lines = mesh.devices.shape
    groups = 8
    planes = wide // groups
    fine = Mesh(mesh.devices.reshape(planes, groups // CORES, CORES, lines), ROW + ("x",))
    in_specs = (
        P("x", ROW, None),
        P("x", ROW, None),
        P(None, ROW),
        P("x", ROW, None),
        P(),
    )
    return jax.shard_map(
        functools.partial(per_device, planes, groups, lines),
        mesh=fine,
        in_specs=in_specs,
        out_specs=P("x", None, ROW),
        check_vma=False,
    )
```

time: 272 us -> 222 us (0.82); the launches traced: 269 us -> 222 us
  blocking collectives: 50 us -> 21 us
  Pallas kernels: 69 us -> 44 us
  waiting for transfers between devices: 117 us -> 97.1 us
  starting transfers between devices: 16.1 us -> 35.5 us
  local copies, waits for them, and re-layouts: 2.38 us -> 8.35 us
    all_gather x3 -> x1, waiting for transfers between devices: 98.3 us -> 0.01 us  [per_device(): maps_basis = lax.all_gather(own, 'z', axis=0)]
    ppermute x3 -> x21, waiting for transfers between devices: 3.09 us -> 81.1 us  [the longest x7 70.6 us: shift(): return lax.ppermute(x, axis, [(i, (i + k) % size) for i in range(size)])]
    all_to_all x2 -> x0, blocking collectives: 35.2 us -> none  [the longest x1 19.6 us: per_device(): lax.all_to_all(part.reshape(groups, rows, sw), ('y', 'c'), 0, 0, tiled=True)]
    pallas_call x4 -> x5, Pallas kernels: 43.5 us -> 21.8 us  [the longest x1 8.75 us: residual_and_sketch(): pl.pallas_call(residual_kernel, grid=(lay, planes // STEP), in_specs=[SCA...]
    ppermute x3 -> x21, starting transfers between devices: 4.85 us -> 24 us  [the longest x14 16.6 us: shift_group(): return lax.ppermute(x, ('y', 'c'), pairs)]
    unnamed x6 -> x12, local copies, waits for them, and re-layouts: 0.71 us -> 7.54 us
    all_to_all x1, blocking collectives: 14.7 us -> 21 us  [per_device(): lax.all_to_all(gram.reshape(planes, sw // planes, sw), 'z', 0, 0, tiled=T...]
    pallas_call x1, Pallas kernels: 25.4 us -> 22.2 us  [inverse_factor(): pl.pallas_call(inverse_factor_kernel, out_shape=jax.ShapeDtypeStruct(gram...]
  transfers between devices with their start and end apart: 9 -> 25, of which waited for: 7 -> 14; matrix products, arithmetic and copies ran while one was open for 1% -> 0% of each run, Pallas kernels for 13% -> 12%
where the time goes in v2:
time: 222 us
  waiting for transfers between devices  97.1 us (44%)
  Pallas kernels  44 us (20%)
  starting transfers between devices  35.5 us (16%)
  blocking collectives  21 us (9%)
  between operations  13.5 us (6%)
  local copies, waits for them, and re-layouts  8.35 us (4%)
    ppermute x7, waiting for transfers between devices, shift(): return lax.ppermute(x, axis, [(i, (i + k) % size) for i in range(size)])  70.6 us
    pallas_call x1, Pallas kernels, inverse_factor(): pl.pallas_call(inverse_factor_kernel, out_shape=jax.ShapeDtypeStruct(gram...  22.2 us
    all_to_all x1, blocking collectives, per_device(): lax.all_to_all(gram.reshape(planes, sw // planes, sw), 'z', 0, 0, tiled=T...  21 us
    ppermute x14, starting transfers between devices, shift_group(): return lax.ppermute(x, ('y', 'c'), pairs)  16.6 us
    all_to_all x1, waiting for transfers between devices, per_device(): lax.all_to_all(jnp.broadcast_to(gram[None], (planes, sw // planes, sw)),...  13.7 us
    ppermute x14, waiting for transfers between devices, shift_group(): return lax.ppermute(x, ('y', 'c'), pairs)  10.4 us
    pallas_call x1, Pallas kernels, residual_and_sketch(): pl.pallas_call(residual_kernel, grid=(lay, planes // STEP), in_specs=[SCA...  8.75 us
    all_to_all x1, starting transfers between devices, per_device(): res_in = lax.all_to_all(cut, ('y', 'c'), 0, 0, tiled=True)  7.89 us
  transfers between devices with their start and end apart: 25, of which 14 were waited for; matrix products, arithmetic and copies ran while one was open for 0% of the time, Pallas kernels for 12%

profile of v2, /device:TPU:1, one launch (start us, length us, event | category | flops | bytes accessed | tf_op | source)
XLA Modules:
  0.0 221.6 jit_solution(10460569245283660474)
XLA Ops:
  6.5 1.9 pad_maximum_fusion.1
  8.4 0.0 all-gather.3.cloned.1.call-update
  8.4 3.6 %cut_by_owner.1 = bf16[8,2,80,2048]{3,2,1,0:T(8,128)(2,1)S(1)} custom-call(bf16[2,80,16384]{2,1,0:T(8,128)(2,1)} %w_ref.1), custom_call_target="tpu_custom_call" | custom-call | tf_op jit(solution)/shard_map/cut_by_owner/pallas_call | solution.py:32
  12.0 2.4 %copy-done = bf16[8,2,80,2048]{3,2,1,0:T(8,128)(2,1)} copy-done((bf16[8,2,80,2048]{3,2,1,0:T(8,128)(2,1)}, bf16[8,2,80,2048]{3,2,1,0:T(8,128)(2,1)S(1)}, u32[]{:S(2)}) %copy-start) | copy-done | bytes 5242904
  14.4 7.9 %all-to-all-start = ((bf16[8,2,80,2048]{3,2,1,0:T(8,128)(2,1)}), bf16[8,2,80,2048]{3,2,1,0:T(8,128)(2,1)}, u32[]{:S(2)}, u32[]{:S(2)}) async-start(bf16[8,2,80,2048]{3,2,1,0:T(8,128)(2,1)} %copy-done), calls=%async_computation | async-start | bytes 10485760 | tf_op jit(solution)/shard_map/all_to_all | solution.py:277
  22.3 1.5 collective-permute-start
  23.7 1.3 collective-permute-start.2
  25.1 1.7 collective-permute-start.1
  26.7 59.0 %collective-permute-done = bf16[2,80,512]{2,1,0:T(8,128)(2,1)S(1)} collective-permute-done((bf16[2,80,512]{2,1,0:T(8,128)(2,1)S(1)}, bf16[2,80,512]{2,1,0:T(8,128)(2,1)S(1)}, u32[]{:S(2)}, u32[]{:S(2)}) %collective-permute-start) | collective-permute-done | bytes 163872 | tf_op jit(solution)/shard_map/ppermute | solution.py:250
  85.7 0.0 collective-permute-done.2
  85.7 3.7 %collective-permute-done.1 = bf16[2,80,512]{2,1,0:T(8,128)(2,1)S(1)} collective-permute-done((bf16[2,80,512]{2,1,0:T(8,128)(2,1)S(1)}, bf16[2,80,512]{2,1,0:T(8,128)(2,1)S(1)}, u32[]{:S(2)}, u32[]{:S(2)}) %collective-permute-start.1) | collective-permute-done | bytes 163872 | tf_op jit(solution)/shard_map/ppermute | solution.py:250
  89.4 0.1 pad_maximum_fusion.c_ref
  89.5 1.0 collective-permute-start.3
  90.4 0.1 pad_add_fusion.pos_ref
  90.5 1.6 collective-permute-done.3.d_ref
  92.2 0.0 all-to-all-done.w_ref
  92.2 2.2 copy-done.1
  94.4 8.7 %residual_and_sketch.1 = (bf16[8,2,80,2048]{3,2,1,0:T(8,128)(2,1)}, f32[80,256]{1,0:T(8,128)S(1)}, f32[80,256]{1,0:T(8,128)S(1)}, f32[80,256]{1,0:T(8,128)S(1)},...) custom-call(s32[2]{0:T(128)S(1)} %pad_add_fusion.pos_ref, ...), custom_call_target="tpu_custom_call" | custom-call | tf_op jit(solution)/shard_map/residual_and_sketch/pallas_call | solution.py:90
  103.1 0.4 collective-permute-start.4
  103.5 0.3 collective-permute-start.5
  103.8 0.1 collective-permute-start.6
  103.8 3.8 %collective-permute-start.7 = (f32[80,256]{1,0:T(8,128)S(1)}, f32[80,256]{1,0:T(8,128)S(1)}, u32[]{:S(2)}, u32[]{:S(2)}) collective-permute-start(f32[80,256]{1,0:T(8,128)S(1)} %get-tuple-element.20), channel_id=1, source_target_pairs={{0,16},{4,20},{8,24},{12,28},{16,0},{20,4},{24,8},{28,12},{1,17},{... | collective-permute-start | bytes 245768 | tf_op jit(solution)/shard_map/ppermute | solution.py:260
  107.7 0.0 collective-permute-start.8
  107.7 0.0 collective-permute-done.4
  107.7 2.3 %collective-permute-start.9 = (f32[80,256]{1,0:T(8,128)S(1)}, f32[80,256]{1,0:T(8,128)S(1)}, u32[]{:S(2)}, u32[]{:S(2)}) collective-permute-start(f32[80,256]{1,0:T(8,128)S(1)} %get-tuple-element.22), channel_id=1, source_target_pairs={{0,24},{4,28},{8,0},{12,4},{16,8},{20,12},{24,16},{28,20},{1,25},{... | collective-permute-start | bytes 245768 | tf_op jit(solution)/shard_map/ppermute | solution.py:260
  110.0 0.0 collective-permute-done.5
  110.0 1.5 collective-permute-start.10
  111.5 2.6 %collective-permute-done.6 = f32[80,256]{1,0:T(8,128)S(1)} collective-permute-done((f32[80,256]{1,0:T(8,128)S(1)}, f32[80,256]{1,0:T(8,128)S(1)}, u32[]{:S(2)}, u32[]{:S(2)}) %collective-permute-start.6) | collective-permute-done | bytes 81952 | tf_op jit(solution)/shard_map/ppermute | solution.py:260
  114.1 0.0 collective-permute-done.7
  114.1 0.0 collective-permute-done.8
  114.1 0.0 collective-permute-done.9
  114.1 1.2 collective-permute-done.10
  115.4 0.8 collective-permute-start.13
  116.2 0.5 collective-permute-start.12
  116.7 0.6 collective-permute-start.11
  117.3 1.9 collective-permute-done.13
  119.2 1.9 collective-permute-done.12
  121.1 2.6 %collective-permute-done.11 = f32[80,256]{1,0:T(8,128)S(1)} collective-permute-done((f32[80,256]{1,0:T(8,128)S(1)}, f32[80,256]{1,0:T(8,128)S(1)}, u32[]{:S(2)}, u32[]{:S(2)}) %collective-permute-start.11) | collective-permute-done | bytes 81952 | tf_op jit(solution)/shard_map/ppermute | solution.py:250
  123.7 3.3 %collective-permute-start.20 = (f32[80,256]{1,0:T(8,128)S(1)}, f32[80,256]{1,0:T(8,128)S(1)}, u32[]{:S(2)}, u32[]{:S(2)}) collective-permute-start(f32[80,256]{1,0:T(8,128)S(1)} %add_add_fusion.refs_0_), channel_id=1, source_target_pairs={{0,28},{4,24},{8,4},{12,0},{16,12},{20,8},{24,20},{28,16},{1,29},{... | collective-permute-start | bytes 245768 | tf_op jit(solution)/shard_map/ppermute | solution.py:260
  127.0 0.0 collective-permute-start.19
  127.0 1.3 collective-permute-start.18
  128.3 2.0 collective-permute-start.17
  130.3 1.7 collective-permute-start.16
  132.0 0.0 collective-permute-done.20.refs_7_
  132.0 0.0 collective-permute-start.15
  132.0 2.4 %collective-permute-done.19.refs_6_ = f32[80,256]{1,0:T(8,128)S(1)} collective-permute-done((f32[80,256]{1,0:T(8,128)S(1)}, f32[80,256]{1,0:T(8,128)S(1)}, u32[]{:S(2)}, u32[]{:S(2)}) %collective-permute-start.19) | collective-permute-done | bytes 81952 | tf_op jit(solution)/shard_map/ppermute | solution.py:260
  134.3 0.0 collective-permute-start.14
  134.4 0.5 collective-permute-done.17.refs_4_
  134.8 1.9 collective-permute-done.16.refs_3_
  136.8 1.8 collective-permute-done.15.refs_2_
  138.5 0.0 collective-permute-done.14.refs_1_
  138.5 1.5 stack_and_gram.1
  140.1 5.9 %project.1 = f32[8,2,256,256]{3,2,1,0:T(8,128)S(1)} custom-call(bf16[512,640]{1,0:T(8,128)(2,1)S(1)} %get-tuple-element.25.both_ref, bf16[8,2,80,2048]{3,2,1,0:T(8,128)(2,1)} %get-tuple-element.26.r_ref), custom_call_target="tpu_custom_call" | custom-call | tf_op jit(solution)/shard_map/project/pallas_call | solution.py:158
  146.0 1.9 copy-done.2
  147.9 0.0 reduce-scatter.2.cloned.1.call-update
  147.9 21.0 %all_to_all.15 = f32[8,32,256]{2,1,0:T(8,128)S(1)} all-to-all(f32[8,32,256]{2,1,0:T(8,128)S(1)} %bitcast.15), channel_id=1, replica_groups=mesh['z'=8,'y'=4,'c'=2,'x'=4] {'z'}, dimensions={0} | all-to-all | bytes 524288 | tf_op jit(solution)/shard_map/all_to_all | solution.py:284
  169.0 0.7 broadcast_in_dim.2
  169.7 3.6 %all-to-all-start.2 = ((f32[8,32,256]{2,1,0:T(8,128)}), f32[8,32,256]{2,1,0:T(8,128)S(1)}, u32[]{:S(2)}, u32[]{:S(2)}) async-start(f32[8,32,256]{2,1,0:T(8,128)} %broadcast_in_dim.2), calls=%async_computation.2 | async-start | bytes 524288 | tf_op jit(solution)/shard_map/all_to_all | solution.py:285
  173.4 0.1 dynamic_slice.3.ranks_ref
  173.4 13.7 %all-to-all-done.2 = f32[8,32,256]{2,1,0:T(8,128)S(1)} async-done(((f32[8,32,256]{2,1,0:T(8,128)}), f32[8,32,256]{2,1,0:T(8,128)S(1)}, u32[]{:S(2)}, u32[]{:S(2)}) %all-to-all-start.2) | async-done | bytes 262176 | tf_op jit(solution)/shard_map/all_to_all | solution.py:285
  187.2 22.2 %inverse_factor.1.inv_ref = f32[256,256]{1,0:T(8,128)S(1)} custom-call(f32[256,256]{1,0:T(8,128)S(1)} %bitcast.13), custom_call_target="tpu_custom_call" | custom-call | tf_op jit(solution)/shard_map/inverse_factor/pallas_call | solution.py:216
  209.4 2.3 %reduce-scatter.2.cloned.1.call-done = f32[1,2,256,256]{3,2,1,0:T(8,128)} async-done(((f32[8,2,256,256]{3,2,1,0:T(8,128)}), f32[1,2,256,256]{3,2,1,0:T(8,128)}) %reduce-scatter.2.cloned.1.call-update) | async-done | bytes 524304 | tf_op jit(solution)/shard_map/reduce_scatter | solution.py:283
  211.7 1.0 copy-done.3
  212.7 2.0 finish.1
  (15 shorter events, 0.1 us)
Async XLA Ops:
  6.5 85.6 %all-gather.3.cloned.1.call-start = ((), (), s32[]{:S(2)}) async-start(), calls=%async_computation.5 | async-start | bytes 4718592 | tf_op jit(solution)/shard_map/all_gather | solution.py:273
  12.0 2.4 %copy-start = (bf16[8,2,80,2048]{3,2,1,0:T(8,128)(2,1)}, bf16[8,2,80,2048]{3,2,1,0:T(8,128)(2,1)S(1)}, u32[]{:S(2)}) copy-start(bf16[8,2,80,2048]{3,2,1,0:T(8,128)(2,1)S(1)} %cut_by_owner.1) | copy-start | bytes 15728644
  14.4 7.9 %copy-start.4 = (bf16[2,80,512]{2,1,0:T(8,128)(2,1)S(1)}, bf16[2,80,512]{2,1,0:T(8,128)(2,1)}, u32[]{:S(2)}) copy-start(bf16[2,80,512]{2,1,0:T(8,128)(2,1)} %param.6) | copy-start | bytes 491524
  14.4 77.8 %all-to-all-start = ((bf16[8,2,80,2048]{3,2,1,0:T(8,128)(2,1)}), bf16[8,2,80,2048]{3,2,1,0:T(8,128)(2,1)}, u32[]{:S(2)}, u32[]{:S(2)}) async-start(bf16[8,2,80,2048]{3,2,1,0:T(8,128)(2,1)} %copy-done), calls=%async_computation | async-start | bytes 10485760 | tf_op jit(solution)/shard_map/all_to_all | solution.py:277
  22.3 189.4 %reduce-scatter.2.cloned.1.call-start = ((), (), s32[]{:S(2)}) async-start(), calls=%async_computation.4 | async-start | bytes 4718592 | tf_op jit(solution)/shard_map/reduce_scatter | solution.py:283
  22.3 63.4 %collective-permute-start = (bf16[2,80,512]{2,1,0:T(8,128)(2,1)S(1)}, bf16[2,80,512]{2,1,0:T(8,128)(2,1)S(1)}, u32[]{:S(2)}, u32[]{:S(2)}) collective-permute-start(bf16[2,80,512]{2,1,0:T(8,128)(2,1)S(1)} %copy-done.4), channel_id=1, source_target_pairs={{0,8},{8,16},{16,24},{24,0},{1,9},{9,17},{17,25},{25,1},{2,10},{10... | collective-permute-start | bytes 491528 | tf_op jit(solution)/shard_map/ppermute | solution.py:250
  23.7 62.0 %collective-permute-start.2 = (bf16[2,80,512]{2,1,0:T(8,128)(2,1)S(1)}, bf16[2,80,512]{2,1,0:T(8,128)(2,1)S(1)}, u32[]{:S(2)}, u32[]{:S(2)}) collective-permute-start(bf16[2,80,512]{2,1,0:T(8,128)(2,1)S(1)} %copy-done.4), channel_id=1, source_target_pairs={{0,24},{8,0},{16,8},{24,16},{1,25},{9,1},{17,9},{25,17},{2,26},{10... | collective-permute-start | bytes 491528 | tf_op jit(solution)/shard_map/ppermute | solution.py:250
  25.1 64.3 %collective-permute-start.1 = (bf16[2,80,512]{2,1,0:T(8,128)(2,1)S(1)}, bf16[2,80,512]{2,1,0:T(8,128)(2,1)S(1)}, u32[]{:S(2)}, u32[]{:S(2)}) collective-permute-start(bf16[2,80,512]{2,1,0:T(8,128)(2,1)S(1)} %copy-done.4), channel_id=1, source_target_pairs={{0,16},{8,24},{16,0},{24,8},{1,17},{9,25},{17,1},{25,9},{2,18},{10... | collective-permute-start | bytes 491528 | tf_op jit(solution)/shard_map/ppermute | solution.py:250
  89.5 2.7 %collective-permute-start.3 = (bf16[4,2,80,512]{3,2,1,0:T(8,128)(2,1)S(1)}, bf16[4,2,80,512]{3,2,1,0:T(8,128)(2,1)S(1)}, u32[]{:S(2)}, u32[]{:S(2)}) collective-permute-start(bf16[4,2,80,512]{3,2,1,0:T(8,128)(2,1)S(1)} %pad_maximum_fusion.c_ref), channel_id=1, source_target_pairs={{0,4},{4,0},{1,5},{5,1},{2,6},{6,2},{3,7},{7,3},{8,12},{12,8},{9,1... | collective-permute-start | bytes 1966088 | tf_op jit(solution)/shard_map/ppermute | solution.py:250
  92.2 2.2 copy-start.1
  103.1 4.6 %collective-permute-start.4 = (f32[80,256]{1,0:T(8,128)S(1)}, f32[80,256]{1,0:T(8,128)S(1)}, u32[]{:S(2)}, u32[]{:S(2)}) collective-permute-start(f32[80,256]{1,0:T(8,128)S(1)} %get-tuple-element.17), channel_id=1, source_target_pairs={{0,4},{4,0},{8,12},{12,8},{16,20},{20,16},{24,28},{28,24},{1,5},{5... | collective-permute-start | bytes 245768 | tf_op jit(solution)/shard_map/ppermute | solution.py:260
  103.5 6.5 %collective-permute-start.5 = (f32[80,256]{1,0:T(8,128)S(1)}, f32[80,256]{1,0:T(8,128)S(1)}, u32[]{:S(2)}, u32[]{:S(2)}) collective-permute-start(f32[80,256]{1,0:T(8,128)S(1)} %get-tuple-element.18), channel_id=1, source_target_pairs={{0,8},{4,12},{8,16},{12,20},{16,24},{20,28},{24,0},{28,4},{1,9},{5... | collective-permute-start | bytes 245768 | tf_op jit(solution)/shard_map/ppermute | solution.py:260
  103.8 10.3 %collective-permute-start.6 = (f32[80,256]{1,0:T(8,128)S(1)}, f32[80,256]{1,0:T(8,128)S(1)}, u32[]{:S(2)}, u32[]{:S(2)}) collective-permute-start(f32[80,256]{1,0:T(8,128)S(1)} %get-tuple-element.19), channel_id=1, source_target_pairs={{0,12},{4,8},{8,20},{12,16},{16,28},{20,24},{24,4},{28,0},{1,13},{... | collective-permute-start | bytes 245768 | tf_op jit(solution)/shard_map/ppermute | solution.py:260
  103.8 10.3 %collective-permute-start.7 = (f32[80,256]{1,0:T(8,128)S(1)}, f32[80,256]{1,0:T(8,128)S(1)}, u32[]{:S(2)}, u32[]{:S(2)}) collective-permute-start(f32[80,256]{1,0:T(8,128)S(1)} %get-tuple-element.20), channel_id=1, source_target_pairs={{0,16},{4,20},{8,24},{12,28},{16,0},{20,4},{24,8},{28,12},{1,17},{... | collective-permute-start | bytes 245768 | tf_op jit(solution)/shard_map/ppermute | solution.py:260
  107.7 6.5 %collective-permute-start.8 = (f32[80,256]{1,0:T(8,128)S(1)}, f32[80,256]{1,0:T(8,128)S(1)}, u32[]{:S(2)}, u32[]{:S(2)}) collective-permute-start(f32[80,256]{1,0:T(8,128)S(1)} %get-tuple-element.21), channel_id=1, source_target_pairs={{0,20},{4,16},{8,28},{12,24},{16,4},{20,0},{24,12},{28,8},{1,21},{... | collective-permute-start | bytes 245768 | tf_op jit(solution)/shard_map/ppermute | solution.py:260
  107.7 6.5 %collective-permute-start.9 = (f32[80,256]{1,0:T(8,128)S(1)}, f32[80,256]{1,0:T(8,128)S(1)}, u32[]{:S(2)}, u32[]{:S(2)}) collective-permute-start(f32[80,256]{1,0:T(8,128)S(1)} %get-tuple-element.22), channel_id=1, source_target_pairs={{0,24},{4,28},{8,0},{12,4},{16,8},{20,12},{24,16},{28,20},{1,25},{... | collective-permute-start | bytes 245768 | tf_op jit(solution)/shard_map/ppermute | solution.py:260
  110.0 5.3 %collective-permute-start.10 = (f32[80,256]{1,0:T(8,128)S(1)}, f32[80,256]{1,0:T(8,128)S(1)}, u32[]{:S(2)}, u32[]{:S(2)}) collective-permute-start(f32[80,256]{1,0:T(8,128)S(1)} %get-tuple-element.23), channel_id=1, source_target_pairs={{0,28},{4,24},{8,4},{12,0},{16,12},{20,8},{24,20},{28,16},{1,29},{... | collective-permute-start | bytes 245768 | tf_op jit(solution)/shard_map/ppermute | solution.py:260
  115.4 3.8 %collective-permute-start.13 = (f32[80,256]{1,0:T(8,128)S(1)}, f32[80,256]{1,0:T(8,128)S(1)}, u32[]{:S(2)}, u32[]{:S(2)}) collective-permute-start(f32[80,256]{1,0:T(8,128)S(1)} %add_add_fusion.1), channel_id=1, source_target_pairs={{0,3},{1,0},{2,1},{3,2},{4,7},{5,4},{6,5},{7,6},{8,11},{9,8},{10,9... | collective-permute-start | bytes 245768 | tf_op jit(solution)/shard_map/ppermute | solution.py:250
  116.2 4.9 %collective-permute-start.12 = (f32[80,256]{1,0:T(8,128)S(1)}, f32[80,256]{1,0:T(8,128)S(1)}, u32[]{:S(2)}, u32[]{:S(2)}) collective-permute-start(f32[80,256]{1,0:T(8,128)S(1)} %add_add_fusion.1), channel_id=1, source_target_pairs={{0,2},{1,3},{2,0},{3,1},{4,6},{5,7},{6,4},{7,5},{8,10},{9,11},{10,... | collective-permute-start | bytes 245768 | tf_op jit(solution)/shard_map/ppermute | solution.py:250
  116.7 6.9 %collective-permute-start.11 = (f32[80,256]{1,0:T(8,128)S(1)}, f32[80,256]{1,0:T(8,128)S(1)}, u32[]{:S(2)}, u32[]{:S(2)}) collective-permute-start(f32[80,256]{1,0:T(8,128)S(1)} %add_add_fusion.1), channel_id=1, source_target_pairs={{0,1},{1,2},{2,3},{3,0},{4,5},{5,6},{6,7},{7,4},{8,9},{9,10},{10,1... | collective-permute-start | bytes 245768 | tf_op jit(solution)/shard_map/ppermute | solution.py:250
  123.7 8.3 %collective-permute-start.20 = (f32[80,256]{1,0:T(8,128)S(1)}, f32[80,256]{1,0:T(8,128)S(1)}, u32[]{:S(2)}, u32[]{:S(2)}) collective-permute-start(f32[80,256]{1,0:T(8,128)S(1)} %add_add_fusion.refs_0_), channel_id=1, source_target_pairs={{0,28},{4,24},{8,4},{12,0},{16,12},{20,8},{24,20},{28,16},{1,29},{... | collective-permute-start | bytes 245768 | tf_op jit(solution)/shard_map/ppermute | solution.py:260
  127.0 7.4 %collective-permute-start.19 = (f32[80,256]{1,0:T(8,128)S(1)}, f32[80,256]{1,0:T(8,128)S(1)}, u32[]{:S(2)}, u32[]{:S(2)}) collective-permute-start(f32[80,256]{1,0:T(8,128)S(1)} %add_add_fusion.refs_0_), channel_id=1, source_target_pairs={{0,24},{4,28},{8,0},{12,4},{16,8},{20,12},{24,16},{28,20},{1,25},{... | collective-permute-start | bytes 245768 | tf_op jit(solution)/shard_map/ppermute | solution.py:260
  127.0 7.4 %collective-permute-start.18 = (f32[80,256]{1,0:T(8,128)S(1)}, f32[80,256]{1,0:T(8,128)S(1)}, u32[]{:S(2)}, u32[]{:S(2)}) collective-permute-start(f32[80,256]{1,0:T(8,128)S(1)} %add_add_fusion.refs_0_), channel_id=1, source_target_pairs={{0,20},{4,16},{8,28},{12,24},{16,4},{20,0},{24,12},{28,8},{1,21},{... | collective-permute-start | bytes 245768 | tf_op jit(solution)/shard_map/ppermute | solution.py:260
  128.3 6.6 %collective-permute-start.17 = (f32[80,256]{1,0:T(8,128)S(1)}, f32[80,256]{1,0:T(8,128)S(1)}, u32[]{:S(2)}, u32[]{:S(2)}) collective-permute-start(f32[80,256]{1,0:T(8,128)S(1)} %add_add_fusion.refs_0_), channel_id=1, source_target_pairs={{0,16},{4,20},{8,24},{12,28},{16,0},{20,4},{24,8},{28,12},{1,17},{... | collective-permute-start | bytes 245768 | tf_op jit(solution)/shard_map/ppermute | solution.py:260
  130.3 6.5 %collective-permute-start.16 = (f32[80,256]{1,0:T(8,128)S(1)}, f32[80,256]{1,0:T(8,128)S(1)}, u32[]{:S(2)}, u32[]{:S(2)}) collective-permute-start(f32[80,256]{1,0:T(8,128)S(1)} %add_add_fusion.refs_0_), channel_id=1, source_target_pairs={{0,12},{4,8},{8,20},{12,16},{16,28},{20,24},{24,4},{28,0},{1,13},{... | collective-permute-start | bytes 245768 | tf_op jit(solution)/shard_map/ppermute | solution.py:260
  132.0 6.6 %collective-permute-start.15 = (f32[80,256]{1,0:T(8,128)S(1)}, f32[80,256]{1,0:T(8,128)S(1)}, u32[]{:S(2)}, u32[]{:S(2)}) collective-permute-start(f32[80,256]{1,0:T(8,128)S(1)} %add_add_fusion.refs_0_), channel_id=1, source_target_pairs={{0,8},{4,12},{8,16},{12,20},{16,24},{20,28},{24,0},{28,4},{1,9},{5... | collective-permute-start | bytes 245768 | tf_op jit(solution)/shard_map/ppermute | solution.py:260
  134.3 4.2 %collective-permute-start.14 = (f32[80,256]{1,0:T(8,128)S(1)}, f32[80,256]{1,0:T(8,128)S(1)}, u32[]{:S(2)}, u32[]{:S(2)}) collective-permute-start(f32[80,256]{1,0:T(8,128)S(1)} %add_add_fusion.refs_0_), channel_id=1, source_target_pairs={{0,4},{4,0},{8,12},{12,8},{16,20},{20,16},{24,28},{28,24},{1,5},{5... | collective-permute-start | bytes 245768 | tf_op jit(solution)/shard_map/ppermute | solution.py:260
  146.0 2.0 copy-start.2
  147.9 25.4 %copy-start.5 = (s32[8]{0:T(128)S(1)}, s32[8]{0:T(128)}, u32[]{:S(2)}) copy-start(s32[8]{0:T(128)} %param.9) | copy-start | bytes 100
  169.7 17.5 %all-to-all-start.2 = ((f32[8,32,256]{2,1,0:T(8,128)}), f32[8,32,256]{2,1,0:T(8,128)S(1)}, u32[]{:S(2)}, u32[]{:S(2)}) async-start(f32[8,32,256]{2,1,0:T(8,128)} %broadcast_in_dim.2), calls=%async_computation.2 | async-start | bytes 524288 | tf_op jit(solution)/shard_map/all_to_all | solution.py:285
  211.7 1.0 copy-start.3
Sparse Core Ops, SparseCore 0:
  9.1 58.6 all-gather.2
  148.1 63.5 reduce-scatter.1
